TPU v7x, 32 devices: a whole 2x2x4 slice. The times are simulated.
32 devices in a mesh: ctx: 8 (over y, x, core), tp: 4 (over z).
Axes of the slice: x: 2, y: 2, z: 4, core: 2. Of those that a mesh axis runs over, the one named last changes fastest.
Arguments:
- queries: bfloat16 [2048, 8192], P('ctx', 'tp'), may hold values from -100 to 100
- key_rows: bfloat16 [2048, 1024], P('ctx'), may hold values from -5 to 5
- value_rows: bfloat16 [2048, 1024], P('ctx'), may hold values from -6 to 6
- documents: int32 [2048], P('ctx'), may hold values from 0 to 3, never falling along the last dimension, each value on 1 to 1536 neighbouring positions
- out_weight: bfloat16 [8192, 8192], P('tp', 'ctx'), may hold values from -0.75 to 0.75
Outputs:
- attention_out: bfloat16 [2048, 8192], P(('ctx', 'tp'))
Inputs may be any that keep to these rules, and one draw needn't show every extreme that they name: `documents`: document numbers never fall along the window; each document holds 1 to 1536 tokens and one holds exactly 1536.
All inputs are finite; a program needn't handle non-finite values.
Results may differ from a plain program's by a relative error of at most 0.015.
Values may be sent and summed in bfloat16 or wider, within the bound.
A program may use at most 128 MiB of HBM per device.

v0:
```python
import functools
import math

import jax
import jax.numpy as jnp
from jax import lax
from jax.experimental import pallas as pl
from jax.experimental.pallas import tpu as pltpu
from jax.sharding import PartitionSpec as P

HEADS = 64
KV_HEADS = 8
HD = 128
DOCS = 4
MESH = pl.DeviceIdType.MESH
F32 = jnp.float32
BF16 = jnp.bfloat16
SCALE2 = math.log2(math.e) / math.sqrt(HD)
UNITS = 4


def fused_kernel(
    q_ref, k_ref, v_ref, drow_ref, w_hbm, out_ref,
    w_ref, kv, docs, k_mask, q_mask, v_down, att, part, zin, fin,
    w_sem, kv_send, kv_recv, doc_send, doc_recv,
    att_send, att_recv, z_send, z_recv, x_send, x_recv,
):
    c = lax.axis_index("ctx")
    z = lax.axis_index("tp")
    ctx = kv.shape[0]
    tokens = q_ref.shape[0]
    rows = att.shape[2]
    kv_here = kv.shape[2] // (2 * HD)
    per_kv = q_ref.shape[1] // HD // kv_here
    unit = part.shape[3]
    width = UNITS * unit

    y, x, core = c // 4, (c // 2) % 2, c % 2

    def at(yy, xx, cc):
        return yy * 4 + xx * 2 + cc

    sib, xn, yn = at(y, x, 1 - core), at(y, 1 - x, core), at(1 - y, x, core)
    dg = at(1 - y, 1 - x, core)
    sib_xn, sib_yn = at(y, 1 - x, 1 - core), at(1 - y, x, 1 - core)
    sib_dg = at(1 - y, 1 - x, 1 - core)

    far = z // 2
    out = 1 - 2 * far
    mid = z * (1 - far) + (3 - z) * far
    ahead, behind = z + out, z - out

    def chunk(p):
        mirrored = (1 - mid) * (3 - p) + mid * (3, 0, 2, 1)[p]
        return mirrored * (1 - far) + (3 - mirrored) * far

    def remote(src, dst, ss, rs, device):
        return pltpu.make_async_remote_copy(
            src_ref=src, dst_ref=dst, send_sem=ss, recv_sem=rs,
            device_id=device, device_id_type=MESH,
        )

    w_copy = pltpu.make_async_copy(w_hbm, w_ref, w_sem)
    w_copy.start()

    barrier = pltpu.get_barrier_semaphore()
    for step in range(1, ctx):
        pl.semaphore_signal(
            barrier, inc=1, device_id=(lax.rem(c + step, ctx), z), device_id_type=MESH
        )
    pl.semaphore_signal(barrier, inc=1, device_id=(c, ahead), device_id_type=MESH)

    @pl.when(mid == 1)
    def _():
        pl.semaphore_signal(barrier, inc=1, device_id=(c, behind), device_id_type=MESH)

    first = pl.multiple_of(z * kv_here * HD, kv_here * HD)
    kv[c, :, : kv_here * HD] = k_ref[:, pl.ds(first, kv_here * HD)]
    kv[c, :, kv_here * HD :] = v_ref[:, pl.ds(first, kv_here * HD)]
    docs[c] = jnp.broadcast_to(drow_ref[...], docs.shape[1:])
    pl.semaphore_wait(barrier, ctx + mid)

    def moves(buf, ss, rs):
        half = buf.shape[1] // 2
        lower, upper = pl.ds(0, half), pl.ds(half, half)
        own = [
            remote(buf.at[c], buf.at[c], ss.at[0], rs.at[0], (sib, z)),
            remote(buf.at[c], buf.at[c], ss.at[1], rs.at[1], (xn, z)),
            remote(buf.at[c], buf.at[c], ss.at[2], rs.at[2], (yn, z)),
        ]
        fwd = [
            remote(buf.at[xn, lower], buf.at[xn, lower], ss.at[3], rs.at[3], (yn, z)),
            remote(buf.at[yn, upper], buf.at[yn, upper], ss.at[4], rs.at[4], (xn, z)),
            remote(buf.at[xn], buf.at[xn], ss.at[5], rs.at[5], (sib, z)),
            remote(buf.at[yn], buf.at[yn], ss.at[6], rs.at[6], (sib, z)),
            remote(buf.at[dg, lower], buf.at[dg, lower], ss.at[7], rs.at[7], (sib, z)),
            remote(buf.at[dg, upper], buf.at[dg, upper], ss.at[8], rs.at[8], (sib, z)),
        ]

        def got(n, view):
            remote(view, view, ss.at[n], rs.at[n], (sib, z)).wait_recv()

        def start_own():
            for copy in own:
                copy.start()

        def forward_near():
            got(1, buf.at[xn])
            fwd[0].start()
            fwd[2].start()
            got(2, buf.at[yn])
            fwd[1].start()
            fwd[3].start()

        def forward_diagonal():
            got(3, buf.at[dg, lower])
            fwd[4].start()
            got(4, buf.at[dg, upper])
            fwd[5].start()

        def all_in():
            got(0, buf.at[sib])
            got(5, buf.at[sib_xn])
            got(6, buf.at[sib_yn])
            got(7, buf.at[sib_dg, lower])
            got(8, buf.at[sib_dg, upper])

        def all_sent():
            for copy in own + fwd:
                copy.wait_send()

        return start_own, forward_near, forward_diagonal, all_in, all_sent

    kv_moves = moves(kv, kv_send, kv_recv)
    kv_moves[0]()
    doc_copies = []
    for step in range(1, ctx):
        peer = lax.rem(c + step, ctx)
        doc_copies.append(
            remote(docs.at[c], docs.at[c], doc_send.at[step], doc_recv.at[step], (peer, z))
        )
        doc_copies[-1].start()
    kv_moves[1]()
    kv_moves[2]()
    for step in range(1, ctx):
        source = lax.rem(c + ctx - step, ctx)
        remote(
            docs.at[source], docs.at[source], doc_send.at[step], doc_recv.at[step], (source, z)
        ).wait_recv()
    kv_moves[3]()

    lane = lax.broadcasted_iota(jnp.int32, (tokens, HD), 1)

    def down(slot):
        across = docs[slot][0:1, :].astype(F32)
        return jnp.broadcast_to(across, (HD, tokens)).T.astype(jnp.int32)

    q_mask[...] = jnp.where(lane == down(c), 1.0, 0.0).astype(BF16)

    def mask_slot(slot, _):
        apart = (lane < DOCS) & (lane != down(slot))
        k_mask[slot] = jnp.where(apart, -(2.0**100), 0.0).astype(BF16)
        for g in range(kv_here):
            v = kv[slot, :, (kv_here + g) * HD : (kv_here + g + 1) * HD]
            v_down[slot, g] = v.astype(F32).T.astype(BF16)
        return 0

    lax.fori_loop(0, ctx, mask_slot, 0)

    pair = 2
    keys = pair * tokens
    blocks = c // pair

    def attend(p):
        t = chunk(p)
        begin = pl.multiple_of(t * rows, rows)
        q_extra = q_mask[pl.ds(begin, rows), :]
        qs = [
            jnp.concatenate(
                [
                    jnp.concatenate(
                        [
                            q_ref[
                                pl.ds(begin, rows),
                                (g * per_kv + h) * HD : (g * per_kv + h + 1) * HD,
                            ],
                            q_extra,
                        ],
                        axis=1,
                    )
                    for h in range(per_kv)
                ],
                axis=0,
            )
            for g in range(kv_here)
        ]

        def body(b, carry, bias=None):
            here = pl.ds(pair * b, pair)
            extra = k_mask[here].reshape(keys, HD)
            ones = jnp.ones((16, keys), BF16)
            state = []
            for g in range(kv_here):
                old_max, acc = carry[g]
                k = kv[here, :, g * HD : (g + 1) * HD].reshape(keys, HD)
                v = jnp.concatenate([v_down[pair * b + n, g] for n in range(pair)], axis=1)
                s = lax.dot_general(
                    jnp.concatenate([k, extra], axis=1), qs[g], (((1,), (1,)), ((), ())),
                    preferred_element_type=F32,
                ) * SCALE2
                if bias is not None:
                    s = s + bias
                new_max = jnp.maximum(old_max, jnp.max(s, axis=0, keepdims=True))
                weights = jnp.exp2(s - new_max).astype(BF16)
                acc = acc * jnp.exp2(old_max - new_max) + jnp.dot(
                    jnp.concatenate([v, ones], axis=0), weights, preferred_element_type=F32
                )
                state.append((new_max, acc))
            return tuple(state)

        lines = per_kv * rows
        state = lax.fori_loop(
            0,
            blocks,
            body,
            ((jnp.full((1, lines), -1e30, F32), jnp.zeros((HD + 16, lines), F32)),) * kv_here,
        )
        line = lax.broadcasted_iota(jnp.int32, (keys, lines), 1)
        q_pos = c * tokens + t * rows + lax.rem(line, rows)
        k_pos = blocks * keys + lax.broadcasted_iota(jnp.int32, (keys, lines), 0)
        state = body(blocks, state, jnp.where(k_pos <= q_pos, 0.0, -1e30).astype(F32))
        for g in range(kv_here):
            acc = state[g][1]
            o = (acc[:HD] / acc[HD : HD + 1]).T.astype(BF16)
            for h in range(per_kv):
                att[p, c, :, (g * per_kv + h) * HD : (g * per_kv + h + 1) * HD] = o[
                    h * rows : (h + 1) * rows
                ]

    def end_hop(p, j):
        return remote(
            part.at[p, j], zin.at[(0, 2, 3)[p], j], z_send.at[p, j],
            z_recv.at[(0, 2, 3)[p], j], (c, ahead),
        )

    def mid_hop(p, j):
        return remote(
            part.at[p, j], zin.at[(1, 0, 4)[p], j], z_send.at[p, j],
            z_recv.at[(1, 0, 4)[p], j], (c, (ahead, behind, ahead)[p]),
        )

    def z_got(slot, j):
        remote(
            zin.at[slot, j], zin.at[slot, j], z_send.at[0, j], z_recv.at[slot, j], (c, ahead)
        ).wait_recv()

    def project(p):
        def body(j, _):
            a = att[p].reshape(ctx * rows, att.shape[3])
            w = w_ref[:, pl.ds(pl.multiple_of(j * unit, unit), unit)]
            part[p, j] = jnp.dot(a, w, preferred_element_type=F32).astype(BF16)
            if p < 3:
                @pl.when(mid == 0)
                def _():
                    end_hop(p, j).start()

            return 0

        lax.fori_loop(0, UNITS, body, 0)

    def pass_on(*units):
        @pl.when(mid == 1)
        def _():
            for p, j in units:
                z_got(p, j)
                part[p, j] = (part[p, j].astype(F32) + zin[p, j].astype(F32)).astype(BF16)
                mid_hop(p, j).start()

    w_copy.wait()
    steps = [
        moves(att.at[p], att_send.at[p], att_recv.at[p]) for p in range(4)
    ]
    attend(0)
    steps[0][0]()
    attend(1)
    steps[0][1]()
    steps[1][0]()
    steps[0][2]()
    steps[0][3]()
    project(0)
    attend(2)
    steps[1][1]()
    steps[2][0]()
    steps[1][2]()
    steps[1][3]()
    project(1)
    pass_on((0, 0))
    attend(3)
    steps[2][1]()
    steps[3][0]()
    steps[2][2]()
    steps[2][3]()
    project(2)
    pass_on((0, 1), (0, 2))
    steps[3][1]()
    steps[3][2]()
    pass_on((1, 0))
    steps[3][3]()
    project(3)
    pass_on((0, 3), (1, 1), (2, 0), (1, 2), (2, 1), (1, 3), (2, 2), (2, 3))

    x_copies = []
    for j in range(UNITS):
        @pl.when(mid == 0)
        def _():
            z_got(0, j)
            total = part[3, j].astype(F32) + zin[0, j].astype(F32)
            fin[j] = total.astype(BF16).reshape(fin.shape[1:])

        @pl.when(mid == 1)
        def _():
            z_got(4, j)
            z_got(3, j)
            total = part[3, j].astype(F32) + zin[3, j].astype(F32) + zin[4, j].astype(F32)
            fin[j] = total.astype(BF16).reshape(fin.shape[1:])

        columns = pl.ds(pl.multiple_of(c * width + j * unit, unit), unit)
        for step in range(1, ctx):
            peer = lax.rem(c + step, ctx)
            x_copies.append(
                remote(
                    fin.at[j, peer], out_ref.at[:, columns], x_send.at[step, j],
                    x_recv.at[step, j], (peer, z),
                )
            )
            x_copies[-1].start()
        out_ref[:, columns] = fin[j, c]

    for j in range(UNITS):
        for step in range(1, ctx):
            source = lax.rem(c + ctx - step, ctx)
            columns = pl.ds(pl.multiple_of(source * width + j * unit, unit), unit)
            remote(
                fin.at[j, source], out_ref.at[:, columns], x_send.at[step, j],
                x_recv.at[step, j], (source, z),
            ).wait_recv()

    kv_moves[4]()
    for copy in doc_copies + x_copies:
        copy.wait_send()
    for step in steps:
        step[4]()

    @pl.when(mid == 0)
    def _():
        for p in range(3):
            for j in range(UNITS):
                end_hop(p, j).wait_send()

    @pl.when(mid == 1)
    def _():
        for p in range(3):
            for j in range(UNITS):
                mid_hop(p, j).wait_send()


def fused(ctx, tp, queries, key_rows, value_rows, documents, out_weight):
    tokens, heads_width = queries.shape
    kv_here = heads_width // HD // (HEADS // KV_HEADS)
    rows = tokens // tp
    depth, width = out_weight.shape
    unit = width // UNITS
    vmem = pl.BlockSpec(memory_space=pltpu.VMEM)
    dma = pltpu.SemaphoreType.DMA
    return pl.pallas_call(
        fused_kernel,
        out_shape=jax.ShapeDtypeStruct((rows, width * ctx), BF16),
        in_specs=[vmem] * 4 + [pl.BlockSpec(memory_space=pl.ANY)],
        out_specs=vmem,
        scratch_shapes=[
            pltpu.VMEM((depth, width), BF16),
            pltpu.VMEM((ctx, tokens, 2 * kv_here * HD), BF16),
            pltpu.VMEM((ctx, 8, tokens), jnp.int32),
            pltpu.VMEM((ctx, tokens, HD), BF16),
            pltpu.VMEM((tokens, HD), BF16),
            pltpu.VMEM((ctx, kv_here, HD, tokens), BF16),
            pltpu.VMEM((tp, ctx, rows, heads_width), BF16),
            pltpu.VMEM((tp, UNITS, ctx * rows, unit), BF16),
            pltpu.VMEM((5, UNITS, ctx * rows, unit), BF16),
            pltpu.VMEM((UNITS, ctx, rows, unit), BF16),
            dma,
            dma((9,)),
            dma((9,)),
            dma((ctx,)),
            dma((ctx,)),
            dma((tp, 9)),
            dma((tp, 9)),
            dma((3, UNITS)),
            dma((5, UNITS)),
            dma((ctx, UNITS)),
            dma((ctx, UNITS)),
        ],
        compiler_params=pltpu.CompilerParams(
            collective_id=0, has_side_effects=True, vmem_limit_bytes=56 * 1024 * 1024
        ),
    )(
        queries, key_rows, value_rows, documents.reshape(1, tokens), out_weight,
    )


def general(ctx, tp, queries, key_rows, value_rows, documents, out_weight):
    tokens = queries.shape[0]
    heads_here = queries.shape[1] // HD
    group_size = HEADS // KV_HEADS
    kv_here = max(1, heads_here // group_size)
    per_kv = heads_here // kv_here
    kv_first = lax.axis_index("tp") * heads_here // group_size
    own_keys = lax.dynamic_slice_in_dim(key_rows, kv_first * HD, kv_here * HD, 1)
    own_values = lax.dynamic_slice_in_dim(value_rows, kv_first * HD, kv_here * HD, 1)
    q = queries.reshape(tokens, kv_here, per_kv, HD)
    keys = lax.all_gather(own_keys, "ctx", axis=0, tiled=True).reshape(-1, kv_here, HD)
    values = lax.all_gather(own_values, "ctx", axis=0, tiled=True).reshape(-1, kv_here, HD)
    docs = lax.all_gather(documents, "ctx", axis=0, tiled=True)
    q_pos = lax.axis_index("ctx") * tokens + jnp.arange(tokens, dtype=jnp.int32)
    k_pos = jnp.arange(keys.shape[0], dtype=jnp.int32)
    allowed = (k_pos[None, :] <= q_pos[:, None]) & (docs[None, :] == documents[:, None])
    scores = jnp.einsum("tghd,ngd->ghtn", q, keys, preferred_element_type=F32) / math.sqrt(HD)
    row_max = jnp.max(jnp.where(allowed, scores, -1e30), axis=3, keepdims=True)
    weights = jnp.where(allowed, jnp.exp(scores - row_max), 0.0)
    total = jnp.transpose(jnp.sum(weights, axis=3), (2, 0, 1))[..., None]
    mixed = jnp.einsum("ghtn,ngd->tghd", weights.astype(BF16), values, preferred_element_type=F32)
    attended = (mixed / total).astype(BF16).reshape(tokens, heads_here * HD)
    gathered = lax.all_gather(attended, "ctx", axis=0, tiled=True)
    terms = jnp.dot(gathered, out_weight, preferred_element_type=F32).astype(BF16)
    terms = jnp.transpose(terms.reshape(ctx, tp, tokens // tp, -1), (1, 0, 2, 3))
    summed = lax.psum_scatter(terms, "tp", scatter_dimension=0, tiled=True)[0]
    return lax.all_to_all(summed, "ctx", split_axis=0, concat_axis=2, tiled=True)[0]


def solution(mesh):
    ctx, tp = mesh.shape["ctx"], mesh.shape["tp"]
    on_device = functools.partial(fused if (ctx, tp) == (8, 4) else general, ctx, tp)
    in_specs = (P("ctx", "tp"), P("ctx", None), P("ctx", None), P("ctx"), P("tp", "ctx"))
    return jax.shard_map(
        on_device, mesh=mesh, in_specs=in_specs,
        out_specs=P(("ctx", "tp"), None), check_vma=False,
    )
```

profile of v0, /device:TPU:9, one launch (start us, length us, event | category | flops | bytes accessed | tf_op | source)
XLA Modules:
  0.0 117.2 jit_solution(3826460259072872612)
XLA Ops:
  0.0 114.9 %shard_map.55 = bf16[64,8192]{1,0:T(8,128)(2,1)} custom-call(bf16[256,2048]{1,0:T(8,128)(2,1)} %q_ref.1, bf16[256,1024]{1,0:T(8,128)(2,1)} %k_ref.1, bf16[256,1024]{1,0:T(8,128)(2,1)} %v_ref.1, s32[1,256]{1,0:T(1,128)} %bitcast.1, bf16[2048,1024]{1,0:T(8,128)(2,1)} %w_hbm.1), custom_call_target="tpu_custom_call" | custom-call | tf_op jit(solution)/shard_map/pallas_call | solution.py:375
  114.9 2.3 %copy.7 = bf16[64,8192]{1,0:T(8,128)(2,1)} copy(bf16[64,8192]{1,0:T(8,128)(2,1)} %shard_map.55) | data formatting | bytes 2097152
where the time goes:
time: 117 us
  Pallas kernels  115 us (98%)
  local copies, waits for them, and re-layouts  2.26 us (2%)
    pallas_call x1, Pallas kernels, fused(): pl.pallas_call(fused_kernel, out_shape=jax.ShapeDtypeStruct((rows, width...  115 us

commit v1 on v0

--- a/solution.py
+++ b/solution.py
@@ -132,7 +132,6 @@
         return start_own, forward_near, forward_diagonal, all_in, all_sent
 
     kv_moves = moves(kv, kv_send, kv_recv)
-    kv_moves[0]()
     doc_copies = []
     for step in range(1, ctx):
         peer = lax.rem(c + step, ctx)
@@ -140,14 +139,12 @@
             remote(docs.at[c], docs.at[c], doc_send.at[step], doc_recv.at[step], (peer, z))
         )
         doc_copies[-1].start()
-    kv_moves[1]()
-    kv_moves[2]()
+    kv_moves[0]()
     for step in range(1, ctx):
         source = lax.rem(c + ctx - step, ctx)
         remote(
             docs.at[source], docs.at[source], doc_send.at[step], doc_recv.at[step], (source, z)
         ).wait_recv()
-    kv_moves[3]()
 
     lane = lax.broadcasted_iota(jnp.int32, (tokens, HD), 1)
 
@@ -160,12 +157,23 @@
     def mask_slot(slot, _):
         apart = (lane < DOCS) & (lane != down(slot))
         k_mask[slot] = jnp.where(apart, -(2.0**100), 0.0).astype(BF16)
-        for g in range(kv_here):
-            v = kv[slot, :, (kv_here + g) * HD : (kv_here + g + 1) * HD]
-            v_down[slot, g] = v.astype(F32).T.astype(BF16)
         return 0
 
     lax.fori_loop(0, ctx, mask_slot, 0)
+
+    def turn(*slots):
+        for slot in slots:
+            for g in range(kv_here):
+                v = kv[slot, :, (kv_here + g) * HD : (kv_here + g + 1) * HD]
+                v_down[slot, g] = v.astype(F32).T.astype(BF16)
+
+    turn(c)
+    kv_moves[1]()
+    turn(xn, yn)
+    kv_moves[2]()
+    turn(dg)
+    kv_moves[3]()
+    turn(sib, sib_xn, sib_yn, sib_dg)
 
     pair = 2
     keys = pair * tokens

time: 117 us -> 118 us (level)
  no operation moved by 1% of the time
where the time goes in v1:
time: 118 us
  Pallas kernels  116 us (98%)
  local copies, waits for them, and re-layouts  2.26 us (2%)
    pallas_call x1, Pallas kernels, fused(): pl.pallas_call(fused_kernel, out_shape=jax.ShapeDtypeStruct((rows, width...  116 us

profile of v1, /device:TPU:9, one launch (start us, length us, event | category | flops | bytes accessed | tf_op | source)
XLA Modules:
  0.0 118.2 jit_solution(4438105431036850356)
XLA Ops:
  0.0 115.9 %shard_map.55 = bf16[64,8192]{1,0:T(8,128)(2,1)} custom-call(bf16[256,2048]{1,0:T(8,128)(2,1)} %q_ref.1, bf16[256,1024]{1,0:T(8,128)(2,1)} %k_ref.1, bf16[256,1024]{1,0:T(8,128)(2,1)} %v_ref.1, s32[1,256]{1,0:T(1,128)} %bitcast.1, bf16[2048,1024]{1,0:T(8,128)(2,1)} %w_hbm.1), custom_call_target="tpu_custom_call" | custom-call | tf_op jit(solution)/shard_map/pallas_call | solution.py:383
  115.9 2.3 %copy.7 = bf16[64,8192]{1,0:T(8,128)(2,1)} copy(bf16[64,8192]{1,0:T(8,128)(2,1)} %shard_map.55) | data formatting | bytes 2097152
